TPU v7x, 512 devices: a whole 4x8x8 slice. The times are simulated.
512 devices in a mesh: member: 16 (over x, y_hi, core), tile: 32 (over z, y_lo).
Axes of the slice: x: 4, y: 8 (y_hi: 2, y_lo: 4; y = y_hi * 4 + y_lo), z: 8, core: 2. Of those that a mesh axis runs over, the one named last changes fastest.
Arguments:
- ensemble: float32 [16, 3, 8, 512, 768], P('member', None, None, 'tile'), may hold values from -6 to 6
- winds: float32 [2, 8, 512, 768], P(None, None, 'tile'), may hold values from -0.35 to 0.35
- diffusion: float32 [8], replicated, may hold values from 0.01 to 0.07
- labels: int32 [512, 768], P('tile'), may hold values from 0 to 15, as said below
- amplitude: float32 [16], replicated, may hold values from 0.5 to 2
Outputs:
- bred: float32 [16, 3, 8, 512, 768], P('member', None, None, 'tile')
Inputs may be any that keep to these rules, and one draw needn't show every extreme that they name: Every region labels at least one column.
All inputs are finite; a program needn't handle non-finite values.
Results may differ from a plain program's by a relative error of at most 0.00017.
Values sent between devices are 32-bit elements; how exact they have to be, the bound alone decides.
A program may use at most 64 MiB of HBM per device.

v0:
```python
import jax
import jax.numpy as jnp
from jax import lax
from jax.sharding import PartitionSpec as P


def padded_2(block, sides, width):
    for axis, dim in sides:
        count = lax.axis_size(axis)
        forward = [(i, i + 1) for i in range(count - 1)]
        forward.append((count - 1, 0))
        backward = [(target, source) for source, target in forward]
        low = lax.ppermute(
            lax.slice_in_dim(block, block.shape[dim] - width, None, axis=dim), axis, forward
        )
        high = lax.ppermute(lax.slice_in_dim(block, 0, width, axis=dim), axis, backward)
        block = jnp.concatenate([low, block, high], axis=dim)
    return block


def spread(block, axis, holder):
    block = jnp.where(lax.axis_index(axis) == holder, block, jnp.zeros_like(block))
    return lax.psum(block, axis)


def stencil(extended, winds, diffusivity):
    centre = extended[..., 1:-1, :]
    western = extended[..., :-2, :]
    eastern = extended[..., 2:, :]
    widths = [(0, 0)] * (centre.ndim - 1) + [(1, 1)]
    padded = jnp.pad(centre, widths)
    southern = padded[..., :-2]
    northern = padded[..., 2:]
    wind_east = winds[0]
    wind_north = winds[1]
    advected = jnp.maximum(wind_east, 0.0) * (centre - western) + jnp.minimum(wind_east, 0.0) * (
        eastern - centre
    )
    advected = (
        advected
        + jnp.maximum(wind_north, 0.0) * (centre - southern)
        + jnp.minimum(wind_north, 0.0) * (northern - centre)
    )
    laplace = western + eastern + southern + northern - 4.0 * centre
    return centre - advected + diffusivity * laplace


def on_device(ensemble, winds, diffusion, labels, amplitude):
    regions = amplitude.shape[0]
    diffusivity = diffusion.reshape(-1, 1, 1)
    fields = ensemble
    for repeat in range(2):
        extended = padded_2(fields, (("tile", 3),), 1)
        fields = stencil(extended, winds, diffusivity)
    perturbed = fields[0]
    control = spread(perturbed, "member", 0)
    departure = perturbed - control
    squares = jnp.sum(departure * departure, axis=(0, 1))
    in_region = labels[None, :, :] == jnp.arange(regions, dtype=jnp.int32)[:, None, None]
    partial_sums = jnp.sum(jnp.where(in_region, squares[None], jnp.float32(0.0)), axis=(1, 2))
    partial_counts = jnp.sum(in_region.astype(jnp.float32), axis=(1, 2))
    sum_squares, counts = lax.psum((partial_sums, partial_counts), "tile")
    levels = ensemble.shape[2]
    fields_count = ensemble.shape[1]
    mean_square = sum_squares / (counts * fields_count * levels)
    factor = amplitude / jnp.sqrt(mean_square + 1e-06)
    column_scale = jnp.sum(jnp.where(in_region, factor[:, None, None], jnp.float32(0.0)), axis=0)
    return (control + departure * column_scale)[None]


def solution(mesh):
    return jax.shard_map(
        on_device,
        mesh=mesh,
        in_specs=(
            P("member", None, None, "tile", None),
            P(None, None, "tile", None),
            P(),
            P("tile", None),
            P(),
        ),
        out_specs=P("member", None, None, "tile", None),
        check_vma=False,
    )
```

profile of v0, /device:TPU:8, one launch (start us, length us, event | category | flops | bytes accessed | tf_op | source)
XLA Modules:
  0.0 316.8 jit_solution(6790023590757075065)
XLA Ops:
  6.5 0.0 all-reduce.5.cloned.1.call-start
  6.5 1.3 fusion.31
  7.9 3.5 %collective-permute-start = (f32[1,3,8,1,768]{4,3,2,1,0:T(1,128)S(1)}, f32[1,3,8,1,768]{4,3,2,1,0:T(1,128)S(1)}, u32[]{:S(2)}, u32[]{:S(2)}) collective-permute-start(f32[1,3,8,1,768]{4,3,2,1,0:T(1,128)S(1)} %get-tuple-element.15), channel_id=1, source_target_pairs={{0,1},{1,2},{2,3},{3,4},{4,5},{5,6},{6,7},{7,8},{8,9},{9,10},{10,1... | collective-permute-start | bytes 221192 | tf_op jit(solution)/shard_map/ppermute | solution.py:13
  11.4 0.0 copy-start.2
  11.4 0.0 copy-start.5
  11.4 6.3 %collective-permute-start.1 = (f32[1,3,8,1,768]{4,3,2,1,0:T(1,128)S(1)}, f32[1,3,8,1,768]{4,3,2,1,0:T(1,128)S(1)}, u32[]{:S(2)}, u32[]{:S(2)}) collective-permute-start(f32[1,3,8,1,768]{4,3,2,1,0:T(1,128)S(1)} %get-tuple-element.16), channel_id=1, source_target_pairs={{1,0},{2,1},{3,2},{4,3},{5,4},{6,5},{7,6},{8,7},{9,8},{10,9},{11,1... | collective-permute-start | bytes 221192 | tf_op jit(solution)/shard_map/ppermute | solution.py:16
  17.7 1.3 maximum_bitcast_fusion.1
  19.0 0.0 collective-permute-done
  19.0 0.7 collective-permute-done.1
  19.7 1.2 fusion.21
  20.9 0.1 fusion.30
  21.0 1.9 collective-permute-start.2
  23.0 8.6 %collective-permute-start.3 = (f32[1,3,8,1,768]{4,3,2,1,0:T(1,128)S(1)}, f32[1,3,8,1,768]{4,3,2,1,0:T(1,128)}, u32[]{:S(2)}, u32[]{:S(2)}) collective-permute-start(f32[1,3,8,1,768]{4,3,2,1,0:T(1,128)S(1)} %get-tuple-element.14), channel_id=1, source_target_pairs={{1,0},{2,1},{3,2},{4,3},{5,4},{6,5},{7,6},{8,7},{9,8},{10,9},{11,1... | collective-permute-start | bytes 221192 | tf_op jit(solution)/shard_map/ppermute | solution.py:16
  31.6 0.4 collective-permute-done.2
  32.0 0.6 copy-done.4
  32.6 0.9 collective-permute-done.3
  33.5 3.3 %broadcast_select_fusion = (f32[3,8,16,768]{3,2,1,0:T(8,128)}, f32[3,8,16,768]{3,2,1,0:T(8,128)S(1)}) fusion(pred[]{:T(512)S(6)} %eq.16, f32[1,3,8,16,768]{4,3,2,1,0:T(8,128)S(1)} %fusion.21, f32[8]{0:T(128)S(1)} %copy-done.5, f32[8,16,768]{2,1,0:T(8,128)S(1)} %get-tuple-element.19, f32[8,16,768]{2,1,0:T(8,128)} %copy-done.1, ...), kind=kLoop, calls=%fused_computation.43 | loop fusion | flops 6488064 | bytes 5259297 | tf_op jit(solution)/shard_map/jit(_where)/select_n | solution.py:22
  36.8 0.0 all-reduce.5.cloned.1.call-update
  36.8 192.7 %all-reduce.5.cloned.1.call-done = f32[3,8,16,768]{3,2,1,0:T(8,128)} async-done(((f32[3,8,16,768]{3,2,1,0:T(8,128)}), f32[3,8,16,768]{3,2,1,0:T(8,128)}) %all-reduce.5.cloned.1.call-update) | async-done | bytes 1179664 | tf_op jit(solution)/shard_map/psum | solution.py:23
  229.5 1.6 multiply_reduce_fusion
  231.1 0.3 convert_reduce_fusion
  231.4 76.4 %all-reduce.2 = (f32[16]{0:T(128)S(1)}, f32[16]{0:T(128)S(1)}) all-reduce(f32[16]{0:T(128)S(1)} %get-tuple-element.6, f32[16]{0:T(128)S(1)} %get-tuple-element.5), channel_id=1, replica_groups=mesh['member'=16,'tile'=32] {'tile'}, use_global_device_ids=true, to_apply=%region_3.4 | all-reduce | flops 32 | bytes 256 | tf_op jit(solution)/shard_map/psum | solution.py:62
  307.8 1.0 select_reduce_fusion
  308.8 1.2 add_bitcast_fusion
  (12 shorter events, 0.0 us)
Async XLA Ops:
  6.5 223.0 %all-reduce.5.cloned.1.call-start = ((), (), s32[]{:S(2)}) async-start(), calls=%async_computation | async-start | bytes 2359296 | tf_op jit(solution)/shard_map/psum | solution.py:23
  7.9 11.1 %collective-permute-start = (f32[1,3,8,1,768]{4,3,2,1,0:T(1,128)S(1)}, f32[1,3,8,1,768]{4,3,2,1,0:T(1,128)S(1)}, u32[]{:S(2)}, u32[]{:S(2)}) collective-permute-start(f32[1,3,8,1,768]{4,3,2,1,0:T(1,128)S(1)} %get-tuple-element.15), channel_id=1, source_target_pairs={{0,1},{1,2},{2,3},{3,4},{4,5},{5,6},{6,7},{7,8},{8,9},{9,10},{10,1... | collective-permute-start | bytes 221192 | tf_op jit(solution)/shard_map/ppermute | solution.py:13
  11.4 8.3 %copy-start.2 = (f32[1,3,8,16,768]{4,3,2,1,0:T(8,128)S(1)}, f32[1,3,8,16,768]{4,3,2,1,0:T(8,128)}, u32[]{:S(2)}) copy-start(f32[1,3,8,16,768]{4,3,2,1,0:T(8,128)} %param.5) | copy-start | bytes 3538948
  11.4 8.3 %copy-start.5 = (f32[8]{0:T(128)S(1)}, f32[8]{0:T(128)}, u32[]{:S(2)}) copy-start(f32[8]{0:T(128)} %param.7) | copy-start | bytes 100
  11.4 8.3 %collective-permute-start.1 = (f32[1,3,8,1,768]{4,3,2,1,0:T(1,128)S(1)}, f32[1,3,8,1,768]{4,3,2,1,0:T(1,128)S(1)}, u32[]{:S(2)}, u32[]{:S(2)}) collective-permute-start(f32[1,3,8,1,768]{4,3,2,1,0:T(1,128)S(1)} %get-tuple-element.16), channel_id=1, source_target_pairs={{1,0},{2,1},{3,2},{4,3},{5,4},{6,5},{7,6},{8,7},{9,8},{10,9},{11,1... | collective-permute-start | bytes 221192 | tf_op jit(solution)/shard_map/ppermute | solution.py:16
  19.0 1.9 copy-start.1
  21.0 10.9 %collective-permute-start.2 = (f32[1,3,8,1,768]{4,3,2,1,0:T(1,128)S(1)}, f32[1,3,8,1,768]{4,3,2,1,0:T(1,128)S(1)}, u32[]{:S(2)}, u32[]{:S(2)}) collective-permute-start(f32[1,3,8,1,768]{4,3,2,1,0:T(1,128)S(1)} %get-tuple-element.13), channel_id=1, source_target_pairs={{0,1},{1,2},{2,3},{3,4},{4,5},{5,6},{6,7},{7,8},{8,9},{9,10},{10,1... | collective-permute-start | bytes 221192 | tf_op jit(solution)/shard_map/ppermute | solution.py:13
  23.0 10.6 %collective-permute-start.3 = (f32[1,3,8,1,768]{4,3,2,1,0:T(1,128)S(1)}, f32[1,3,8,1,768]{4,3,2,1,0:T(1,128)}, u32[]{:S(2)}, u32[]{:S(2)}) collective-permute-start(f32[1,3,8,1,768]{4,3,2,1,0:T(1,128)S(1)} %get-tuple-element.14), channel_id=1, source_target_pairs={{1,0},{2,1},{3,2},{4,3},{5,4},{6,5},{7,6},{8,7},{9,8},{10,9},{11,1... | collective-permute-start | bytes 221192 | tf_op jit(solution)/shard_map/ppermute | solution.py:16
  32.0 0.6 copy-start.4
  229.5 1.6 copy-start.3
  229.5 78.3 %copy-start.6 = (f32[16]{0:T(128)S(1)}, f32[16]{0:T(128)}, u32[]{:S(2)}) copy-start(f32[16]{0:T(128)} %param.9) | copy-start | bytes 196
  229.5 79.2 %copy-start = (f32[3,8,16,768]{3,2,1,0:T(8,128)S(1)}, f32[3,8,16,768]{3,2,1,0:T(8,128)}, u32[]{:S(2)}) copy-start(f32[3,8,16,768]{3,2,1,0:T(8,128)} %all-reduce.5.cloned.1.call-done) | copy-start | bytes 3538948
Sparse Core Ops, SparseCore 0:
  36.9 192.5 all-reduce.4
where the time goes:
time: 317 us
  waiting for transfers between devices  195 us (62%)
  blocking collectives  76.4 us (24%)
  starting transfers between devices  20.3 us (6%)
  between operations  13.5 us (4%)
  other arithmetic  9.72 us (3%)
    psum x1, waiting for transfers between devices, spread(): return lax.psum(block, axis)  193 us
    psum x1, blocking collectives, on_device(): sum_squares, counts = lax.psum((partial_sums, partial_counts), 'tile')  76.4 us
    ppermute x2, starting transfers between devices, padded_2(): lax.ppermute(lax.slice_in_dim(block, 0, width, axis=dim), axis, backward)  14.9 us
  transfers between devices with their start and end apart: 5, of which 4 were waited for; matrix products, arithmetic and copies ran while one was open for 0% of the time, Pallas kernels for 0%

commit v1 on v0

v1 whole, which is shorter than its diff:
```python
import functools

import jax
import jax.numpy as jnp
from jax import lax
from jax.experimental import pallas as pl
from jax.experimental.pallas import tpu as pltpu
from jax.sharding import PartitionSpec as P

MESH = pl.DeviceIdType.MESH
DMA = pltpu.SemaphoreType.DMA
TILES = 32
PAD = 8


def kernel(
    ens, winds, diffusion, labels, amplitude, ctl, dep, scale,
    ext, wext, coef, mid, acc, ar,
    load_sem, halo_send, halo_recv, s1_send, s1_recv, cross_send, cross_recv,
    s2_send, s2_recv, sib_send, sib_recv, ar_send, ar_recv,
):
    fields, levels, rows, cols = ctl.shape
    regions = amplitude.shape[0]
    m = lax.axis_index("member")
    t = lax.axis_index("tile")
    x, yh, c = m // 4, (m // 2) % 2, m % 2
    mine = 2 * x + c
    sib = m + 1 - 2 * c
    other_half = m + 2 - 4 * yh

    def mate(k):
        return (m + 4 * k) % 16

    def tile(d):
        return (t + d) % TILES

    def remote(src, dst, send, recv, member, at):
        return pltpu.make_async_remote_copy(
            src_ref=src, dst_ref=dst, send_sem=send, recv_sem=recv,
            device_id=(member, at), device_id_type=MESH,
        )

    own_rows = pl.ds(PAD, rows)
    load_f = pltpu.make_async_copy(ens.at[0], ext.at[:, :, own_rows], load_sem.at[0])
    load_w = pltpu.make_async_copy(winds, wext.at[:, :, own_rows], load_sem.at[1])
    load_f.start()
    load_w.start()

    barrier = pltpu.get_barrier_semaphore()
    near = [mate(1), mate(2), mate(3), sib, other_half]
    near += [(sib + 4 * k) % 16 for k in (1, 2, 3)]
    for member in near:
        pl.semaphore_signal(barrier, inc=1, device_id=(member, t), device_id_type=MESH)
    for d in range(1, TILES):
        pl.semaphore_signal(barrier, inc=1, device_id=(m, tile(d)), device_id_type=MESH)
    pl.semaphore_wait(barrier, len(near) + TILES - 1)

    halos = [
        remote(ens.at[0, :, :, pl.ds(rows - 2, 2)], ext.at[:, :, pl.ds(PAD - 2, 2)],
               halo_send.at[0], halo_recv.at[0], m, tile(1)),
        remote(ens.at[0, :, :, pl.ds(0, 2)], ext.at[:, :, pl.ds(PAD + rows, 2)],
               halo_send.at[1], halo_recv.at[1], m, tile(TILES - 1)),
        remote(winds.at[:, :, pl.ds(rows - 1, 1)], wext.at[:, :, pl.ds(PAD - 1, 1)],
               halo_send.at[2], halo_recv.at[2], m, tile(1)),
        remote(winds.at[:, :, pl.ds(0, 1)], wext.at[:, :, pl.ds(PAD + rows, 1)],
               halo_send.at[3], halo_recv.at[3], m, tile(TILES - 1)),
    ]
    for copy in halos:
        copy.start()
    load_f.wait()
    load_w.wait()
    for copy in halos:
        copy.wait_recv()

    column = lax.broadcasted_iota(jnp.int32, (rows + 2 * PAD, cols), 1)

    def stencil(v, c0, cw, ce, cs, cn):
        n = v.shape[0]
        return (
            c0 * v
            + cw * pltpu.roll(v, 1, 0)
            + ce * pltpu.roll(v, n - 1, 0)
            + cs * pltpu.roll(v, 1, 1)
            + cn * pltpu.roll(v, cols - 1, 1)
        )

    def s1(level):
        holder = (level // 2) * 4 + level % 2
        return remote(dep.at[:, level], ctl.at[:, level], s1_send.at[level], s1_recv, holder, t)

    def advance(level, carry):
        east, north = wext[0, level], wext[1, level]
        k = diffusion[level]
        east_p, east_m = jnp.maximum(east, 0.0), jnp.minimum(east, 0.0)
        north_p, north_m = jnp.maximum(north, 0.0), jnp.minimum(north, 0.0)
        coef[0] = 1.0 - east_p + east_m - north_p + north_m - 4.0 * k
        coef[1] = east_p + k
        coef[2] = k - east_m
        coef[3] = jnp.where(column == 0, 0.0, north_p + k)
        coef[4] = jnp.where(column == cols - 1, 0.0, k - north_m)
        for f in range(fields):
            mid[...] = stencil(ext[f, level], *(coef[i] for i in range(5)))
            new = stencil(mid[...], *(coef[i] for i in range(5)))
            dep[f, level] = new[PAD:PAD + rows]

        @pl.when((m == 0) & (level > 0))
        def _():
            s1(level).start()

        return carry

    lax.fori_loop(0, levels, advance, 0)

    @pl.when(m == 0)
    def _():
        ctl[:, 0] = dep[:, 0]

    @pl.when((m != 0) & (yh == 0))
    def _():
        s1(mine).wait_recv()

    cross = remote(ctl.at[:, mine], ctl.at[:, mine], cross_send, cross_recv, other_half, t)

    @pl.when(yh == 0)
    def _():
        cross.start()

    @pl.when(yh == 1)
    def _():
        cross.wait_recv()

    def from_x(k, core):
        return 2 * ((x + 4 - k) % 4) + core

    def s2(k):
        return remote(ctl.at[:, mine], ctl.at[:, mine], s2_send.at[k], s2_recv.at[k], mate(k), t)

    def s2_arrival(k):
        level = from_x(k, c)
        return remote(ctl.at[:, level], ctl.at[:, level], s2_send.at[k], s2_recv.at[k], mate(k), t)

    def to_sib(k):
        level = from_x(k, c)
        return remote(ctl.at[:, level], ctl.at[:, level], sib_send.at[k], sib_recv.at[k], sib, t)

    def from_sib(k):
        level = from_x(k, 1 - c)
        return remote(ctl.at[:, level], ctl.at[:, level], sib_send.at[k], sib_recv.at[k], sib, t)

    @pl.when(m == 0)
    def _():
        for level in range(1, levels):
            s1(level).wait_send()

    for k in (2, 1, 3):
        s2(k).start()
    to_sib(0).start()
    acc[...] = jnp.zeros_like(acc)

    def add_squares(level):
        total = acc[...]
        for f in range(fields):
            d = dep[f, level] - ctl[f, level]
            dep[f, level] = d
            total = total + d * d
        acc[...] = total

    add_squares(mine)
    for k in (1, 3, 2):
        s2_arrival(k).wait_recv()
        to_sib(k).start()
        add_squares(from_x(k, c))
    for k in (0, 1, 3, 2):
        from_sib(k).wait_recv()
        add_squares(from_x(k, 1 - c))

    lane = lax.broadcasted_iota(jnp.int32, (8, 128), 1)
    sub = lax.broadcasted_iota(jnp.int32, (8, 128), 0)
    block = jnp.zeros((8, 128), jnp.float32)
    squares = acc[...]
    where_label = labels[...]
    target = jnp.zeros((8, 128), jnp.float32)
    for r in range(regions):
        hit = where_label == r
        total = jnp.sum(jnp.where(hit, squares, 0.0))
        count = jnp.sum(hit.astype(jnp.float32))
        row, at = sub == r % 8, r // 8
        block = jnp.where(row & (lane == at), total, block)
        block = jnp.where(row & (lane == at + 2), count, block)
        target = jnp.where(row & (lane == at), amplitude[r], target)
    ar[0] = block

    def ar_copy(d):
        return remote(ar.at[0], ar.at[d], ar_send, ar_recv, m, tile(d))

    for d in range(1, TILES):
        ar_copy(d).start()
    rest = ar.at[pl.ds(1, TILES - 1)]
    pltpu.make_async_copy(rest, rest, ar_recv).wait()
    total = jnp.sum(ar[...], axis=0)
    counts = pltpu.roll(total, 126, 1)
    counts = jnp.where(lane < 2, counts, 1.0)
    factor = target / jnp.sqrt(total / (counts * (fields * levels)) + 1e-06)
    scales = jnp.zeros((rows, cols), jnp.float32)
    for r in range(regions):
        value = factor[r % 8:r % 8 + 1, r // 8:r // 8 + 1]
        scales = jnp.where(where_label == r, value, scales)
    scale[...] = scales

    pltpu.make_async_copy(rest, rest, ar_send).wait()
    for copy in halos:
        copy.wait_send()

    @pl.when(yh == 0)
    def _():
        cross.wait_send()

    for k in (1, 2, 3):
        s2(k).wait_send()
    for k in range(4):
        to_sib(k).wait_send()


def on_device(ensemble, winds, diffusion, labels, amplitude):
    _, fields, levels, rows, cols = ensemble.shape
    block = jax.ShapeDtypeStruct((fields, levels, rows, cols), jnp.float32)
    f32 = jnp.float32
    tall = rows + 2 * PAD
    vmem = pl.BlockSpec(memory_space=pltpu.VMEM)
    smem = pl.BlockSpec(memory_space=pltpu.SMEM)
    hbm = pl.BlockSpec(memory_space=pl.ANY)
    control, departure, scale = pl.pallas_call(
        kernel,
        name="breed",
        out_shape=(block, block, jax.ShapeDtypeStruct((rows, cols), f32)),
        in_specs=[hbm, hbm, smem, vmem, smem],
        out_specs=(vmem, vmem, vmem),
        scratch_shapes=[
            pltpu.VMEM((fields, levels, tall, cols), f32),
            pltpu.VMEM((2, levels, tall, cols), f32),
            pltpu.VMEM((5, tall, cols), f32),
            pltpu.VMEM((tall, cols), f32),
            pltpu.VMEM((rows, cols), f32),
            pltpu.VMEM((TILES, 8, 128), f32),
            DMA((2,)), DMA((4,)), DMA((4,)), DMA((levels,)), DMA, DMA, DMA,
            DMA((4,)), DMA((4,)), DMA((4,)), DMA((4,)), DMA, DMA,
        ],
        compiler_params=pltpu.CompilerParams(
            collective_id=0, has_side_effects=True, vmem_limit_bytes=32 * 2**20
        ),
    )(ensemble, winds, diffusion, labels, amplitude)
    return (control + departure * scale)[None]


def solution(mesh):
    return jax.shard_map(
        on_device,
        mesh=mesh,
        in_specs=(
            P("member", None, None, "tile", None),
            P(None, None, "tile", None),
            P(),
            P("tile", None),
            P(),
        ),
        out_specs=P("member", None, None, "tile", None),
        check_vma=False,
    )
```

time: 317 us -> 66 us (0.21)
  the two profiles are of different devices: /device:TPU:8 before, /device:TPU:62 now
where the time goes in v1:
time: 66 us; the launch traced here: 65.8 us
  Pallas kernels  60.1 us (91%)
  local copies, waits for them, and re-layouts  4.51 us (7%)
  other arithmetic  1.16 us (2%)
    pallas_call x1, Pallas kernels, on_device(): pl.pallas_call(kernel, name='breed', out_shape=(block, block, jax.ShapeDt...  60.1 us
    unnamed x10, local copies, waits for them, and re-layouts  4.51 us

profile of v1, /device:TPU:62, one launch (start us, length us, event | category | flops | bytes accessed | tf_op | source)
XLA Modules:
  0.0 65.8 jit_solution(2003925922581216820)
XLA Ops:
  0.0 0.0 copy-start
  0.0 1.3 %copy-done = f32[1,3,8,16,768]{4,3,2,1,0:T(8,128)S(1)} copy-done((f32[1,3,8,16,768]{4,3,2,1,0:T(8,128)S(1)}, f32[1,3,8,16,768]{4,3,2,1,0:T(8,128)}, u32[]{:S(2)}) %copy-start) | copy-done | bytes 1179672
  1.3 0.0 copy-start.1
  1.3 1.1 %copy-done.1 = f32[2,8,16,768]{3,2,1,0:T(8,128)S(1)} copy-done((f32[2,8,16,768]{3,2,1,0:T(8,128)S(1)}, f32[2,8,16,768]{3,2,1,0:T(8,128)}, u32[]{:S(2)}) %copy-start.1) | copy-done | bytes 786456
  2.4 0.0 copy-start.2
  2.4 0.8 %copy-done.2 = s32[16,768]{1,0:T(8,128)S(1)} copy-done((s32[16,768]{1,0:T(8,128)S(1)}, s32[16,768]{1,0:T(8,128)}, u32[]{:S(2)}) %copy-start.2) | copy-done | bytes 49176
  3.2 0.0 copy-start.3
  3.2 0.7 copy-done.3
  3.9 0.0 copy-start.4
  3.9 0.7 copy-done.4
  4.5 60.1 %breed.1 = (f32[3,8,16,768]{3,2,1,0:T(8,128)S(1)}, f32[3,8,16,768]{3,2,1,0:T(8,128)S(1)}, f32[16,768]{1,0:T(8,128)S(1)}) custom-call(f32[1,3,8,16,768]{4,3,2,1,0:T(8,128)S(1)} %copy-done, f32[2,8,16,768]{3,2,1,0:T(8,128)S(1)} %copy-done.1, f32[8]{0:T(128)S(1)} %copy-done.3, s32[16,768]{1,0:T(8,128)S(1)} %copy-done.2, f32[16]{0:T(128)S(1)} %copy-done.4), custom_call_target="tpu_custom_call" | custom-call | tf_op jit(solution)/shard_map/breed/pallas_call | solution.py:232
  64.6 1.2 %add_bitcast_fusion = f32[1,3,8,16,768]{4,3,2,1,0:T(8,128)} fusion(f32[3,8,16,768]{3,2,1,0:T(8,128)S(1)} %get-tuple-element.8, f32[3,8,16,768]{3,2,1,0:T(8,128)S(1)} %get-tuple-element.9, f32[16,768]{1,0:T(8,128)S(1)} %get-tuple-element.10), kind=kLoop, calls=%fused_computation | loop fusion | flops 589824 | bytes 3588096 | tf_op jit(solution)/shard_map/broadcast_in_dim | solution.py:252
Async XLA Ops:
  0.0 1.3 %copy-start = (f32[1,3,8,16,768]{4,3,2,1,0:T(8,128)S(1)}, f32[1,3,8,16,768]{4,3,2,1,0:T(8,128)}, u32[]{:S(2)}) copy-start(f32[1,3,8,16,768]{4,3,2,1,0:T(8,128)} %ens.1) | copy-start | bytes 3538948
  1.3 1.1 %copy-start.1 = (f32[2,8,16,768]{3,2,1,0:T(8,128)S(1)}, f32[2,8,16,768]{3,2,1,0:T(8,128)}, u32[]{:S(2)}) copy-start(f32[2,8,16,768]{3,2,1,0:T(8,128)} %winds.1) | copy-start | bytes 2359300
  2.4 0.8 %copy-start.2 = (s32[16,768]{1,0:T(8,128)S(1)}, s32[16,768]{1,0:T(8,128)}, u32[]{:S(2)}) copy-start(s32[16,768]{1,0:T(8,128)} %labels.1) | copy-start | bytes 147460
  3.2 0.7 copy-start.3
  3.9 0.7 copy-start.4

commit v2 on v1

v2 whole, which is shorter than its diff:
```python
import jax
import jax.numpy as jnp
from jax import lax
from jax.experimental import pallas as pl
from jax.experimental.pallas import tpu as pltpu
from jax.sharding import PartitionSpec as P

MESH = pl.DeviceIdType.MESH
DMA = pltpu.SemaphoreType.DMA
TILES = 32


def kernel(
    ens, winds, diffusion_in, labels_in, amplitude_in, ctl, dep, scale,
    ext, wext, cext, coef, mid, acc, ar, diffusion, labels, amplitude,
    load_sem, halo_send, halo_recv, s1_send, s1_recv, cross_send, cross_recv,
    s2_send, s2_recv, sib_send, sib_recv, edge_send, edge_recv,
    e2_send, e2_recv, esib_send, esib_recv, ar_send, ar_recv,
):
    fields, levels, rows, cols = ctl.shape
    tall = ext.shape[2]
    regions = amplitude.shape[0]
    m = lax.axis_index("member")
    t = lax.axis_index("tile")
    x, yh, c = m // 4, (m // 2) % 2, m % 2
    mine = 2 * x + c
    sib = m + 1 - 2 * c
    other_half = m + 2 - 4 * yh
    every = range(fields)

    def mate(k):
        return (m + 4 * k) % 16

    def tile(d):
        return (t + d) % TILES

    def remote(src, dst, send, recv, member, at):
        return pltpu.make_async_remote_copy(
            src_ref=src, dst_ref=dst, send_sem=send, recv_sem=recv,
            device_id=(member, at), device_id_type=MESH,
        )

    own = pl.ds(0, rows)
    loads = [
        pltpu.make_async_copy(ens.at[0], ext.at[:, :, own], load_sem.at[0]),
        pltpu.make_async_copy(winds, wext.at[:, :, own], load_sem.at[1]),
        pltpu.make_async_copy(diffusion_in, diffusion, load_sem.at[2]),
        pltpu.make_async_copy(labels_in, labels, load_sem.at[3]),
        pltpu.make_async_copy(amplitude_in, amplitude, load_sem.at[4]),
    ]
    for copy in loads:
        copy.start()
    root_load = pltpu.make_async_copy(ens.at[0, :, 0], cext.at[:, 0, own], load_sem.at[5])

    @pl.when(m == 0)
    def _():
        root_load.start()

    barrier = pltpu.get_barrier_semaphore()
    near = [mate(1), mate(2), mate(3), sib, other_half]
    near += [(sib + 4 * k) % 16 for k in (1, 2, 3)]
    for d in range(1, TILES):
        pl.semaphore_signal(barrier, inc=1, device_id=(m, tile(d)), device_id_type=MESH)
    for member in near:
        pl.semaphore_signal(barrier, inc=1, device_id=(member, t), device_id_type=MESH)
    pl.semaphore_wait(barrier, len(near) + TILES - 1)

    def s1(level, f):
        holder = (level // 2) * 4 + level % 2
        return remote(ens.at[0, f, level], cext.at[f, level, own],
                      s1_send.at[level, f], s1_recv.at[f], holder, t)

    @pl.when(m == 0)
    def _():
        for f in every:
            for level in (4, 5, 2, 3, 6, 7, 1):
                s1(level, f).start()

    last, first = pl.ds(rows - 2, 2), pl.ds(0, 2)
    low, high = pl.ds(tall - 2, 2), pl.ds(rows, 2)
    halos = [
        remote(winds.at[:, :, pl.ds(rows - 1, 1)], wext.at[:, :, pl.ds(tall - 1, 1)],
               halo_send.at[2], halo_recv.at[2], m, tile(1)),
        remote(winds.at[:, :, pl.ds(0, 1)], wext.at[:, :, pl.ds(rows, 1)],
               halo_send.at[3], halo_recv.at[3], m, tile(TILES - 1)),
        remote(ens.at[0, :, :, last], ext.at[:, :, low],
               halo_send.at[0], halo_recv.at[0], m, tile(1)),
        remote(ens.at[0, :, :, first], ext.at[:, :, high],
               halo_send.at[1], halo_recv.at[1], m, tile(TILES - 1)),
    ]
    for copy in halos:
        copy.start()

    def cross(f):
        at = cext.at[f, mine, own]
        return remote(at, at, cross_send.at[f], cross_recv.at[f], other_half, t)

    def level_of(k, core):
        return 2 * ((x + 4 - k) % 4) + core

    def s2(k, f):
        at = cext.at[f, mine, own]
        return remote(at, at, s2_send.at[k, f], s2_recv.at[k, f], mate(k), t)

    def s2_in(k, f):
        at = cext.at[f, level_of(k, c), own]
        return remote(at, at, s2_send.at[k, f], s2_recv.at[k, f], mate(k), t)

    def to_sib(k, f):
        at = cext.at[f, level_of(k, c), own]
        return remote(at, at, sib_send.at[k, f], sib_recv.at[k, f], sib, t)

    def from_sib(k, f):
        at = cext.at[f, level_of(k, 1 - c), own]
        return remote(at, at, sib_send.at[k, f], sib_recv.at[k, f], sib, t)

    @pl.when(m == 0)
    def _():
        root_load.wait()

    for f in every:
        @pl.when((m != 0) & (yh == 0))
        def _():
            s1(mine, f).wait_recv()

        @pl.when(yh == 0)
        def _():
            cross(f).start()

        @pl.when(yh == 1)
        def _():
            cross(f).wait_recv()

        for k in (2, 1, 3):
            s2(k, f).start()
        to_sib(0, f).start()

    edges = [
        remote(cext.at[:, mine, last], cext.at[:, mine, low],
               edge_send.at[0], edge_recv.at[0], m, tile(1)),
        remote(cext.at[:, mine, first], cext.at[:, mine, high],
               edge_send.at[1], edge_recv.at[1], m, tile(TILES - 1)),
    ]
    for copy in edges:
        copy.start()

    for copy in loads:
        copy.wait()
    for copy in halos[:2]:
        copy.wait_recv()

    column = lax.broadcasted_iota(jnp.int32, (tall, cols), 1)

    def weigh(level, carry):
        east, north = wext[0, level], wext[1, level]
        k = diffusion[level]
        east_p, east_m = jnp.maximum(east, 0.0), jnp.minimum(east, 0.0)
        north_p, north_m = jnp.maximum(north, 0.0), jnp.minimum(north, 0.0)
        coef[level, 0] = 1.0 - east_p + east_m - north_p + north_m - 4.0 * k
        coef[level, 1] = east_p + k
        coef[level, 2] = k - east_m
        coef[level, 3] = jnp.where(column == 0, 0.0, north_p + k)
        coef[level, 4] = jnp.where(column == cols - 1, 0.0, k - north_m)
        return carry

    lax.fori_loop(0, levels, weigh, 0)

    def step(v, level):
        return (
            coef[level, 0] * v
            + coef[level, 1] * pltpu.roll(v, 1, 0)
            + coef[level, 2] * pltpu.roll(v, tall - 1, 0)
            + coef[level, 3] * pltpu.roll(v, 1, 1)
            + coef[level, 4] * pltpu.roll(v, cols - 1, 1)
        )

    def two_steps(v, level):
        mid[...] = step(v, level)
        return step(mid[...], level)[:rows]

    for copy in halos[2:]:
        copy.wait_recv()

    def advance(level, carry):
        for f in every:
            dep[f, level] = two_steps(ext[f, level], level)
        return carry

    lax.fori_loop(0, levels, advance, 0)

    for f in every:
        for k in (1, 3, 2):
            s2_in(k, f).wait_recv()
            to_sib(k, f).start()

    def e2(k, side):
        at = cext.at[:, mine, (low, high)[side]]
        return remote(at, at, e2_send.at[k, side], e2_recv.at[k, side], mate(k), t)

    def e2_in(k, side):
        at = cext.at[:, level_of(k, c), (low, high)[side]]
        return remote(at, at, e2_send.at[k, side], e2_recv.at[k, side], mate(k), t)

    def edge_to_sib(k, side):
        at = cext.at[:, level_of(k, c), (low, high)[side]]
        return remote(at, at, esib_send.at[k, side], esib_recv.at[k, side], sib, t)

    def edge_from_sib(k, side):
        at = cext.at[:, level_of(k, 1 - c), (low, high)[side]]
        return remote(at, at, esib_send.at[k, side], esib_recv.at[k, side], sib, t)

    for side in (0, 1):
        edges[side].wait_recv()
        for k in (2, 1, 3):
            e2(k, side).start()
        edge_to_sib(0, side).start()

    acc[...] = jnp.zeros_like(acc)

    def depart(level):
        def one(f, carry):
            control = two_steps(cext[f, level], level)
            d = dep[f, level] - control
            ctl[f, level] = control
            dep[f, level] = d
            acc[...] = acc[...] + d * d
            return carry

        lax.fori_loop(0, fields, one, 0)

    depart(mine)
    for k in (1, 3, 2):
        for side in (0, 1):
            e2_in(k, side).wait_recv()
            edge_to_sib(k, side).start()
        depart(level_of(k, c))
    for k in (0, 1, 3, 2):
        for f in every:
            from_sib(k, f).wait_recv()
        for side in (0, 1):
            edge_from_sib(k, side).wait_recv()
        depart(level_of(k, 1 - c))

    lane = lax.broadcasted_iota(jnp.int32, (8, 128), 1)
    sub = lax.broadcasted_iota(jnp.int32, (8, 128), 0)
    block = jnp.zeros((8, 128), jnp.float32)
    squares = acc[...]
    where_label = labels[...]
    target = jnp.zeros((8, 128), jnp.float32)
    for r in range(regions):
        hit = where_label == r
        total = jnp.sum(jnp.where(hit, squares, 0.0))
        count = jnp.sum(hit.astype(jnp.float32))
        row, at = sub == r % 8, r // 8
        block = jnp.where(row & (lane == at), total, block)
        block = jnp.where(row & (lane == at + 2), count, block)
        target = jnp.where(row & (lane == at), amplitude[r], target)
    ar[0] = block

    def ar_copy(d):
        return remote(ar.at[0], ar.at[d], ar_send, ar_recv, m, tile(d))

    for d in range(1, TILES):
        ar_copy(d).start()
    rest = ar.at[pl.ds(1, TILES - 1)]
    pltpu.make_async_copy(rest, rest, ar_recv).wait()
    total = jnp.sum(ar[...], axis=0)
    counts = pltpu.roll(total, 126, 1)
    counts = jnp.where(lane < 2, counts, 1.0)
    factor = target / jnp.sqrt(total / (counts * (fields * levels)) + 1e-06)
    scales = jnp.zeros((rows, cols), jnp.float32)
    for r in range(regions):
        value = factor[r % 8:r % 8 + 1, r // 8:r // 8 + 1]
        scales = jnp.where(where_label == r, value, scales)
    scale[...] = scales

    pltpu.make_async_copy(rest, rest, ar_send).wait()
    for copy in halos + edges:
        copy.wait_send()
    for f in every:
        @pl.when(m == 0)
        def _():
            for level in range(1, levels):
                s1(level, f).wait_send()

        @pl.when(yh == 0)
        def _():
            cross(f).wait_send()

        for k in (1, 2, 3):
            s2(k, f).wait_send()
        for k in range(4):
            to_sib(k, f).wait_send()
    for side in (0, 1):
        for k in (1, 2, 3):
            e2(k, side).wait_send()
        for k in range(4):
            edge_to_sib(k, side).wait_send()


def on_device(ensemble, winds, diffusion, labels, amplitude):
    _, fields, levels, rows, cols = ensemble.shape
    block = jax.ShapeDtypeStruct((fields, levels, rows, cols), jnp.float32)
    f32 = jnp.float32
    tall = rows + 8
    vmem = pl.BlockSpec(memory_space=pltpu.VMEM)
    hbm = pl.BlockSpec(memory_space=pltpu.HBM)
    inputs = [
        pltpu.with_memory_space_constraint(a, pltpu.HBM)
        for a in (ensemble, winds, diffusion, labels, amplitude)
    ]
    pair = (DMA((4, 2)), DMA((4, 2)))
    control, departure, scale = pl.pallas_call(
        kernel,
        name="breed",
        out_shape=(block, block, jax.ShapeDtypeStruct((rows, cols), f32)),
        in_specs=[hbm] * 5,
        out_specs=(vmem, vmem, vmem),
        scratch_shapes=[
            pltpu.VMEM((fields, levels, tall, cols), f32),
            pltpu.VMEM((2, levels, tall, cols), f32),
            pltpu.VMEM((fields, levels, tall, cols), f32),
            pltpu.VMEM((levels, 5, tall, cols), f32),
            pltpu.VMEM((tall, cols), f32),
            pltpu.VMEM((rows, cols), f32),
            pltpu.VMEM((TILES, 8, 128), f32),
            pltpu.SMEM((levels,), f32),
            pltpu.VMEM((rows, cols), jnp.int32),
            pltpu.SMEM(amplitude.shape, f32),
            DMA((6,)), DMA((4,)), DMA((4,)), DMA((levels, fields)), DMA((fields,)),
            DMA((fields,)), DMA((fields,)),
            DMA((4, fields)), DMA((4, fields)), DMA((4, fields)), DMA((4, fields)),
            DMA((2,)), DMA((2,)), *pair, *pair, DMA, DMA,
        ],
        compiler_params=pltpu.CompilerParams(
            collective_id=0, has_side_effects=True, vmem_limit_bytes=32 * 2**20
        ),
    )(*inputs)
    return (control + departure * scale)[None]


def solution(mesh):
    return jax.shard_map(
        on_device,
        mesh=mesh,
        in_specs=(
            P("member", None, None, "tile", None),
            P(None, None, "tile", None),
            P(),
            P("tile", None),
            P(),
        ),
        out_specs=P("member", None, None, "tile", None),
        check_vma=False,
    )
```

time: 66 us -> 52.9 us (0.80)
  the two profiles are of different devices: /device:TPU:62 before, /device:TPU:56 now
where the time goes in v2:
time: 52.9 us; the launch traced here: 52.8 us
  Pallas kernels  51.6 us (98%)
  other arithmetic  1.16 us (2%)
    pallas_call x1, Pallas kernels, on_device(): pl.pallas_call(kernel, name='breed', out_shape=(block, block, jax.ShapeDt...  51.6 us
    broadcast_in_dim x1, other arithmetic, on_device(): return (control + departure * scale)[None]  1.16 us

profile of v2, /device:TPU:56, one launch (start us, length us, event | category | flops | bytes accessed | tf_op | source)
XLA Modules:
  0.0 52.8 jit_solution(7741816911377341528)
XLA Ops:
  0.0 51.6 %breed.1 = (f32[3,8,16,768]{3,2,1,0:T(8,128)S(1)}, f32[3,8,16,768]{3,2,1,0:T(8,128)S(1)}, f32[16,768]{1,0:T(8,128)S(1)}) custom-call(f32[1,3,8,16,768]{4,3,2,1,0:T(8,128)} %ens.1, f32[2,8,16,768]{3,2,1,0:T(8,128)} %winds.1, f32[8]{0:T(128)} %diffusion_in.1, s32[16,768]{1,0:T(8,128)} %labels_in.1, f32[16]{0:T(128)} %amplitude_in.1), custom_call_target="tpu_custom_call" | custom-call | tf_op jit(solution)/shard_map/breed/pallas_call | solution.py:313
  51.6 1.2 %add_bitcast_fusion = f32[1,3,8,16,768]{4,3,2,1,0:T(8,128)} fusion(f32[3,8,16,768]{3,2,1,0:T(8,128)S(1)} %get-tuple-element.8, f32[3,8,16,768]{3,2,1,0:T(8,128)S(1)} %get-tuple-element.9, f32[16,768]{1,0:T(8,128)S(1)} %get-tuple-element.10), kind=kLoop, calls=%fused_computation | loop fusion | flops 589824 | bytes 3588096 | tf_op jit(solution)/shard_map/broadcast_in_dim | solution.py:339

commit v3 on v2

v3 whole, which is shorter than its diff:
```python
import jax
import jax.numpy as jnp
from jax import lax
from jax.experimental import pallas as pl
from jax.experimental.pallas import tpu as pltpu
from jax.sharding import PartitionSpec as P

MESH = pl.DeviceIdType.MESH
DMA = pltpu.SemaphoreType.DMA
TILES = 32


def kernel(
    ens, winds, diffusion_in, labels_in, amplitude_in, ctl, dep, scale,
    ext, wext, cext, cown, fix, coef, mid, acc, rim, part, ar, diffusion, labels, amplitude,
    load_sem, halo_send, halo_recv, wind_send, wind_recv,
    root_send, pair_send, pair_recv, hop_send, cross_send, s2_send, sib_send, main_recv,
    edge_send, edge_recv, e2_send, e2_recv, esib_send, esib_recv, ar_send, ar_recv,
):
    fields, levels, rows, cols = ctl.shape
    tall = ext.shape[2]
    regions = amplitude.shape[0]
    m = lax.axis_index("member")
    t = lax.axis_index("tile")
    x, yh, c = m // 4, (m // 2) % 2, m % 2
    mine = 2 * x + c
    sib = m + 1 - 2 * c
    other_half = m + 2 - 4 * yh
    every = range(fields)

    def mate(k):
        return (m + 4 * k) % 16

    def tile(d):
        return (t + d) % TILES

    def remote(src, dst, send, recv, member, at):
        return pltpu.make_async_remote_copy(
            src_ref=src, dst_ref=dst, send_sem=send, recv_sem=recv,
            device_id=(member, at), device_id_type=MESH,
        )

    own = pl.ds(0, rows)
    loads = [
        pltpu.make_async_copy(ens.at[0], ext.at[:, :, own], load_sem.at[0]),
        pltpu.make_async_copy(winds, wext.at[:, :, own], load_sem.at[1]),
        pltpu.make_async_copy(diffusion_in, diffusion, load_sem.at[2]),
        pltpu.make_async_copy(labels_in, labels, load_sem.at[3]),
        pltpu.make_async_copy(amplitude_in, amplitude, load_sem.at[4]),
    ]
    for copy in loads:
        copy.start()
    root_load = pltpu.make_async_copy(ens.at[0], cext, load_sem.at[5])

    @pl.when(m == 0)
    def _():
        root_load.start()

    barrier = pltpu.get_barrier_semaphore()
    near = [mate(1), mate(2), mate(3), sib, other_half, sib + 2 - 4 * yh]
    near += [(sib + 4 * k) % 16 for k in (1, 2, 3)]
    for member in near:
        pl.semaphore_signal(barrier, inc=1, device_id=(member, t), device_id_type=MESH)
    for d in range(1, TILES):
        pl.semaphore_signal(barrier, inc=1, device_id=(m, tile(d)), device_id_type=MESH)
    pl.semaphore_wait(barrier, len(near) + TILES - 1)

    def up(core):
        return [(2, 0), (2 * (1 - core), 1), (1, 0), (1, 1), (1, 2), (0, 0)]

    def down(core):
        return [(2, 2), (2 * core, 1), (3, 0), (3, 1), (3, 2), (0, 2)]

    def plane(f, level):
        return cext.at[f, level]

    def arrival(f, level):
        at = plane(f, level)
        return remote(at, at, hop_send.at[f, level], main_recv.at[f, level], sib, t)

    def pass_on(f, level, member):
        at = plane(f, level)
        return remote(at, at, hop_send.at[f, level], main_recv.at[f, level], member, t)

    def cross(f):
        at = plane(f, mine)
        return remote(at, at, cross_send.at[0, f], main_recv.at[f, mine], other_half, t)

    def to_sib(f, level):
        at = plane(f, level)
        return remote(at, at, sib_send.at[f, level], main_recv.at[f, level], sib, t)

    def root_chain(f, level, member):
        return remote(ens.at[0, f, level], plane(f, level),
                      root_send.at[f, level], main_recv.at[f, level], member, t)

    def root_cross(f, level):
        return remote(ens.at[0, f, level], plane(f, level),
                      cross_send.at[level, f], main_recv.at[f, level], 2 + level, t)

    def root_pair(f):
        return remote(ens.at[0, f], cext.at[f], pair_send.at[f], pair_recv.at[f], 1, t)

    @pl.when(m == 0)
    def _():
        for i in range(6):
            for core in (0, 1):
                q, f = up(core)[i]
                root_chain(f, 2 * q + core, 4 + core).start()
                q, f = down(core)[i]
                root_chain(f, 2 * q + core, 12 + core).start()
            if i < fields:
                for core in (0, 1):
                    root_cross(i, core).start()
        for f in every:
            root_pair(f).start()

    last, first = pl.ds(rows - 2, 2), pl.ds(0, 2)
    low, high = pl.ds(tall - 2, 2), pl.ds(rows, 2)
    wind_last, wind_first = pl.ds(rows - 1, 1), pl.ds(0, 1)
    wind_low, wind_high = pl.ds(tall - 1, 1), pl.ds(rows, 1)
    halos = [
        remote(winds.at[c, :, wind_last], wext.at[c, :, wind_low],
               halo_send.at[2], halo_recv.at[2], m, tile(1)),
        remote(winds.at[c, :, wind_first], wext.at[c, :, wind_high],
               halo_send.at[3], halo_recv.at[3], m, tile(TILES - 1)),
        remote(ens.at[0, :, :, last], ext.at[:, :, low],
               halo_send.at[0], halo_recv.at[0], m, tile(1)),
        remote(ens.at[0, :, :, first], ext.at[:, :, high],
               halo_send.at[1], halo_recv.at[1], m, tile(TILES - 1)),
    ]
    for copy in halos:
        copy.start()

    def level_of(k, core):
        return 2 * ((x + 4 - k) % 4) + core

    def s2(k, f):
        at = plane(f, mine)
        return remote(at, at, s2_send.at[k, f], main_recv.at[f, mine], mate(k), t)

    edges = [
        remote(cext.at[:, mine, last], cown.at[:, low],
               edge_send.at[0], edge_recv.at[0], m, tile(1)),
        remote(cext.at[:, mine, first], cown.at[:, high],
               edge_send.at[1], edge_recv.at[1], m, tile(TILES - 1)),
    ]
    def start_edges():
        for copy in edges:
            copy.start()

    def along(plane_of, member):
        q, f = plane_of
        level = 2 * q + c
        arrival(f, level).wait_recv()
        if member is not None:
            pass_on(f, level, member).start()
        to_sib(f, level).start()

    @pl.when(m == 0)
    def _():
        root_load.wait()
        start_edges()

    @pl.when(m == 1)
    def _():
        for f in every:
            root_pair(f).wait_recv()
        start_edges()

    @pl.when((yh == 0) & (x == 1))
    def _():
        for i, p in enumerate(up(c)):
            along(p, 8 + c)
            if 2 <= i < 5:
                cross(i - 2).start()
            if i == 4:
                start_edges()
        for p in down(c):
            along(p, None)

    @pl.when((yh == 0) & (x == 3))
    def _():
        for i, p in enumerate(down(c)):
            along(p, 8 + c)
            if 2 <= i < 5:
                cross(i - 2).start()
            if i == 4:
                start_edges()
        for p in up(c):
            along(p, None)

    @pl.when((yh == 0) & (x == 2))
    def _():
        for i, (p, n) in enumerate(zip(up(c), down(c))):
            along(p, 12 + c)
            if i == 0:
                cross(0).start()
            along(n, 4 + c)
            if i == 0:
                cross(2).start()
            if i == 1:
                cross(1).start()
                start_edges()

    @pl.when(yh == 1)
    def _():
        for f in every:
            arrival(f, mine).wait_recv()
            for k in (2, 1, 3):
                s2(k, f).start()
            to_sib(f, mine).start()
        start_edges()

    for copy in loads:
        copy.wait()
    wind_pair = [
        remote(wext.at[c, :, at], wext.at[c, :, at], wind_send.at[i], wind_recv.at[i], sib, t)
        for i, at in enumerate((wind_low, wind_high))
    ]
    for copy, pair in zip(halos[:2], wind_pair):
        copy.wait_recv()
        pair.start()
    for i, at in enumerate((wind_low, wind_high)):
        there = wext.at[1 - c, :, at]
        remote(there, there, wind_send.at[i], wind_recv.at[i], sib, t).wait_recv()

    column = lax.broadcasted_iota(jnp.int32, (tall, cols), 1)

    def weigh(level, carry):
        east, north = wext[0, level], wext[1, level]
        k = diffusion[level]
        east_p, east_m = jnp.maximum(east, 0.0), jnp.minimum(east, 0.0)
        north_p, north_m = jnp.maximum(north, 0.0), jnp.minimum(north, 0.0)
        coef[level, 0] = 1.0 - east_p + east_m - north_p + north_m - 4.0 * k
        coef[level, 1] = east_p + k
        coef[level, 2] = k - east_m
        coef[level, 3] = jnp.where(column == 0, 0.0, north_p + k)
        coef[level, 4] = jnp.where(column == cols - 1, 0.0, k - north_m)
        return carry

    lax.fori_loop(0, levels, weigh, 0)

    def step(v, level):
        n = v.shape[0]
        return (
            coef[level, 0, :n] * v
            + coef[level, 1, :n] * pltpu.roll(v, 1, 0)
            + coef[level, 2, :n] * pltpu.roll(v, n - 1, 0)
            + coef[level, 3, :n] * pltpu.roll(v, 1, 1)
            + coef[level, 4, :n] * pltpu.roll(v, cols - 1, 1)
        )

    def two_steps(v, level):
        n = v.shape[0]
        mid[:n] = step(v, level)
        return step(mid[:n], level)[:rows]

    for copy in halos[2:]:
        copy.wait_recv()

    sub = lax.broadcasted_iota(jnp.int32, (8, cols), 0)
    acc[...] = jnp.zeros_like(acc)

    def advance(level, carry):
        for f in every:
            new = two_steps(ext[f, level], level)
            dep[f, level] = new
            rim[f, level] = jnp.where(sub < 4, new[:8], new[8:])
        return carry

    lax.fori_loop(0, levels, advance, 0)

    def gather(f):
        @pl.when(yh == 1)
        def _():
            for k in (1, 3, 2):
                arrival(f, level_of(k, c)).wait_recv()
                to_sib(f, level_of(k, c)).start()

    gather(0)
    gather(1)

    def rows_of(ref, level, side):
        if ref is fix:
            return fix.at[:, level, (pl.ds(0, 2), pl.ds(6, 2))[side]]
        return ctl.at[:, level, (first, last)[side]]

    def e2(k, side):
        return remote(rows_of(ctl, mine, side), rows_of(fix, mine, side),
                      e2_send.at[k, side], e2_recv.at[k, side], mate(k), t)

    def e2_in(k, side):
        at = rows_of(fix, level_of(k, c), side)
        return remote(at, at, e2_send.at[k, side], e2_recv.at[k, side], mate(k), t)

    def edge_to_sib(k, side):
        level = level_of(k, c)
        return remote(rows_of(fix if k else ctl, level, side), rows_of(fix, level, side),
                      esib_send.at[k, side], esib_recv.at[k, side], sib, t)

    def edge_from_sib(k, side):
        at = rows_of(fix, level_of(k, 1 - c), side)
        return remote(at, at, esib_send.at[k, side], esib_recv.at[k, side], sib, t)

    for side in (0, 1):
        edges[side].wait_recv()

    def own_level(f, carry):
        cown[f, :rows] = cext[f, mine]
        control = two_steps(cown[f], mine)
        ctl[f, mine] = control
        fix[f, mine] = jnp.where(sub < 4, control[:8], control[8:])
        d = dep[f, mine] - control
        dep[f, mine] = d
        acc[...] = acc[...] + d * d
        return carry

    lax.fori_loop(0, fields, own_level, 0)
    for side in (0, 1):
        for k in (2, 1, 3):
            e2(k, side).start()
        edge_to_sib(0, side).start()

    def other_levels(f):
        @pl.when((yh == 1) | (x > 0))
        def _():
            for k in range(4):
                arrival(f, level_of(k, 1 - c)).wait_recv()

        def one(i, carry):
            level = (mine + 1 + i) % levels
            control = two_steps(cext[f, level], level)
            ctl[f, level] = control
            d = dep[f, level] - control
            dep[f, level] = d
            acc[...] = acc[...] + d * d
            return carry

        lax.fori_loop(0, levels - 1, one, 0)

    other_levels(0)
    other_levels(1)
    gather(2)
    other_levels(2)

    def blocks(v):
        return sum(v[:, 128 * i:128 * (i + 1)] for i in range(cols // 128))

    def along_lanes(offset):
        sums = jnp.sum(jnp.sum(part[...], axis=1), axis=1, keepdims=True)
        lane = lax.broadcasted_iota(jnp.int32, (regions, 128), 1)
        region = lax.broadcasted_iota(jnp.int32, (regions, 128), 0)
        return jnp.sum(jnp.where(lane == region + offset, sums, 0.0), axis=0, keepdims=True)

    lane = lax.broadcasted_iota(jnp.int32, (1, 128), 1)
    target = jnp.zeros((1, 128), jnp.float32)
    outer = (sub < 2) | (sub >= 6)
    where_label = labels[...]
    for r in range(regions):
        one = (where_label == r).astype(jnp.float32)
        part[r] = blocks(one[:8] + one[8:])
        target = jnp.where(lane == r, amplitude[r], target)
    counts = along_lanes(regions)
    top = jnp.where(sub < 2, 0.0, acc[:8])
    bottom = jnp.where(sub >= 6, 0.0, acc[8:])
    for r in range(regions):
        part[r] = blocks(
            jnp.where(where_label[:8] == r, top, 0.0) + jnp.where(where_label[8:] == r, bottom, 0.0)
        )

    def depart(level, total):
        for f in every:
            d = rim[f, level] - fix[f, level]
            total = total + d * d
        return total

    total = depart(mine, jnp.zeros((8, cols), jnp.float32))
    for k in (1, 3, 2):
        for side in (0, 1):
            e2_in(k, side).wait_recv()
            edge_to_sib(k, side).start()
        total = depart(level_of(k, c), total)
    for k in (0, 1, 3, 2):
        for side in (0, 1):
            edge_from_sib(k, side).wait_recv()
        total = depart(level_of(k, 1 - c), total)
    label_rim = jnp.where(sub < 4, where_label[:8], where_label[8:])
    label_rim = jnp.where(outer, label_rim, -1)
    for r in range(regions):
        part[r] = part[r] + blocks(jnp.where(label_rim == r, total, 0.0))
    ar[0] = along_lanes(0) + counts

    def ar_copy(d):
        return remote(ar.at[0], ar.at[d], ar_send, ar_recv, m, tile(d))

    far_first = sorted(range(1, TILES), key=lambda d: abs(d - TILES // 2))
    for d in far_first:
        ar_copy(d).start()

    def patch(i, carry):
        level = (mine + 1 + i) % levels
        for f in every:
            edge = fix[f, level]
            d = rim[f, level] - edge
            ctl[f, level, :8] = jnp.where(sub < 2, edge, ctl[f, level, :8])
            ctl[f, level, 8:] = jnp.where(sub >= 6, edge, ctl[f, level, 8:])
            dep[f, level, :8] = jnp.where(sub < 2, d, dep[f, level, :8])
            dep[f, level, 8:] = jnp.where(sub >= 6, d, dep[f, level, 8:])
        return carry

    lax.fori_loop(0, levels - 1, patch, 0)
    rest = ar.at[pl.ds(1, TILES - 1)]
    pltpu.make_async_copy(rest, rest, ar_recv).wait()
    total = jnp.sum(ar[...], axis=0)
    counts = pltpu.roll(total, 128 - regions, 1)
    counts = jnp.where(lane < regions, counts, 1.0)
    factor = target / jnp.sqrt(total / (counts * (fields * levels)) + 1e-06)
    scales = jnp.zeros((rows, cols), jnp.float32)
    for r in range(regions):
        scales = jnp.where(where_label == r, factor[:, r:r + 1], scales)
    scale[...] = scales

    pltpu.make_async_copy(rest, rest, ar_send).wait()
    for copy in halos + edges + wind_pair:
        copy.wait_send()

    @pl.when(m == 0)
    def _():
        for f in every:
            for level in range(levels):
                root_chain(f, level, 4).wait_send()
            for core in (0, 1):
                root_cross(f, core).wait_send()
            root_pair(f).wait_send()

    @pl.when((yh == 1) | (x > 0))
    def _():
        for f in every:
            for k in range(4):
                to_sib(f, 2 * k + c).wait_send()

    @pl.when((yh == 0) & (x > 0))
    def _():
        for f in every:
            cross(f).wait_send()

    @pl.when((yh == 0) & ((x == 1) | (x == 2)))
    def _():
        for q, f in up(c):
            pass_on(f, 2 * q + c, sib).wait_send()

    @pl.when((yh == 0) & ((x == 3) | (x == 2)))
    def _():
        for q, f in down(c):
            pass_on(f, 2 * q + c, sib).wait_send()

    @pl.when(yh == 1)
    def _():
        for f in every:
            for k in (1, 2, 3):
                s2(k, f).wait_send()

    for side in (0, 1):
        for k in (1, 2, 3):
            e2(k, side).wait_send()
        for k in range(4):
            edge_to_sib(k, side).wait_send()


def on_device(ensemble, winds, diffusion, labels, amplitude):
    _, fields, levels, rows, cols = ensemble.shape
    block = jax.ShapeDtypeStruct((fields, levels, rows, cols), jnp.float32)
    f32 = jnp.float32
    tall = rows + 8
    vmem = pl.BlockSpec(memory_space=pltpu.VMEM)
    hbm = pl.BlockSpec(memory_space=pltpu.HBM)
    inputs = [
        pltpu.with_memory_space_constraint(a, pltpu.HBM)
        for a in (ensemble, winds, diffusion, labels, amplitude)
    ]
    pair = (DMA((4, 2)), DMA((4, 2)))
    planes = DMA((fields, levels))
    control, departure, scale = pl.pallas_call(
        kernel,
        name="breed",
        out_shape=(block, block, jax.ShapeDtypeStruct((rows, cols), f32)),
        in_specs=[hbm] * 5,
        out_specs=(vmem, vmem, vmem),
        scratch_shapes=[
            pltpu.VMEM((fields, levels, tall, cols), f32),
            pltpu.VMEM((2, levels, tall, cols), f32),
            pltpu.VMEM((fields, levels, rows, cols), f32),
            pltpu.VMEM((fields, tall, cols), f32),
            pltpu.VMEM((fields, levels, 8, cols), f32),
            pltpu.VMEM((levels, 5, tall, cols), f32),
            pltpu.VMEM((tall, cols), f32),
            pltpu.VMEM((rows, cols), f32),
            pltpu.VMEM((fields, levels, 8, cols), f32),
            pltpu.VMEM((amplitude.shape[0], 8, 128), f32),
            pltpu.VMEM((TILES, 1, 128), f32),
            pltpu.SMEM((levels,), f32),
            pltpu.VMEM((rows, cols), jnp.int32),
            pltpu.SMEM(amplitude.shape, f32),
            DMA((6,)), DMA((4,)), DMA((4,)), DMA((2,)), DMA((2,)),
            planes, DMA((fields,)), DMA((fields,)), planes, DMA((2, fields)),
            DMA((4, fields)), planes, planes,
            DMA((2,)), DMA((2,)), *pair, *pair, DMA, DMA,
        ],
        compiler_params=pltpu.CompilerParams(
            collective_id=0, has_side_effects=True, vmem_limit_bytes=32 * 2**20
        ),
    )(*inputs)
    return (control + departure * scale)[None]


def solution(mesh):
    return jax.shard_map(
        on_device,
        mesh=mesh,
        in_specs=(
            P("member", None, None, "tile", None),
            P(None, None, "tile", None),
            P(),
            P("tile", None),
            P(),
        ),
        out_specs=P("member", None, None, "tile", None),
        check_vma=False,
    )
```

time: 52.9 us -> 51.2 us (0.968)
  Pallas kernels: 51.6 us -> 49.9 us
    pallas_call x1, Pallas kernels: 51.6 us -> 49.9 us  [on_device(): pl.pallas_call(kernel, name='breed', out_shape=(block, block, jax.ShapeDt...]
where the time goes in v3:
time: 51.2 us; the launch traced here: 51 us
  Pallas kernels  49.9 us (97%)
  other arithmetic  1.16 us (2%)
    pallas_call x1, Pallas kernels, on_device(): pl.pallas_call(kernel, name='breed', out_shape=(block, block, jax.ShapeDt...  49.9 us
    broadcast_in_dim x1, other arithmetic, on_device(): return (control + departure * scale)[None]  1.16 us

profile of v3, /device:TPU:56, one launch (start us, length us, event | category | flops | bytes accessed | tf_op | source)
XLA Modules:
  0.0 51.0 jit_solution(9553938647297833712)
XLA Ops:
  0.0 49.9 %breed.1 = (f32[3,8,16,768]{3,2,1,0:T(8,128)S(1)}, f32[3,8,16,768]{3,2,1,0:T(8,128)S(1)}, f32[16,768]{1,0:T(8,128)S(1)}) custom-call(f32[1,3,8,16,768]{4,3,2,1,0:T(8,128)} %ens.1, f32[2,8,16,768]{3,2,1,0:T(8,128)} %winds.1, f32[8]{0:T(128)} %diffusion_in.1, s32[16,768]{1,0:T(8,128)} %labels_in.1, f32[16]{0:T(128)} %amplitude_in.1), custom_call_target="tpu_custom_call" | custom-call | tf_op jit(solution)/shard_map/breed/pallas_call | solution.py:484
  49.9 1.2 %add_bitcast_fusion = f32[1,3,8,16,768]{4,3,2,1,0:T(8,128)} fusion(f32[3,8,16,768]{3,2,1,0:T(8,128)S(1)} %get-tuple-element.8, f32[3,8,16,768]{3,2,1,0:T(8,128)S(1)} %get-tuple-element.9, f32[16,768]{1,0:T(8,128)S(1)} %get-tuple-element.10), kind=kLoop, calls=%fused_computation | loop fusion | flops 589824 | bytes 3588096 | tf_op jit(solution)/shard_map/broadcast_in_dim | solution.py:514

commit v4 on v3

--- a/solution.py
+++ b/solution.py
@@ -279,7 +279,6 @@
                 to_sib(f, level_of(k, c)).start()
 
     gather(0)
-    gather(1)
 
     def rows_of(ref, level, side):
         if ref is fix:
@@ -339,6 +338,7 @@
 
         lax.fori_loop(0, levels - 1, one, 0)
 
+    gather(1)
     other_levels(0)
     other_levels(1)
     gather(2)

time: 51.2 us -> 50.6 us (0.988)
  Pallas kernels: 49.9 us -> 49.2 us
    pallas_call x1, Pallas kernels: 49.9 us -> 49.2 us  [on_device(): pl.pallas_call(kernel, name='breed', out_shape=(block, block, jax.ShapeDt...]
where the time goes in v4:
time: 50.6 us; the launch traced here: 50.4 us
  Pallas kernels  49.2 us (97%)
  other arithmetic  1.16 us (2%)
    pallas_call x1, Pallas kernels, on_device(): pl.pallas_call(kernel, name='breed', out_shape=(block, block, jax.ShapeDt...  49.2 us
    broadcast_in_dim x1, other arithmetic, on_device(): return (control + departure * scale)[None]  1.16 us

profile of v4, /device:TPU:56, one launch (start us, length us, event | category | flops | bytes accessed | tf_op | source)
XLA Modules:
  0.0 50.4 jit_solution(2022418646019489847)
XLA Ops:
  0.0 49.2 %breed.1 = (f32[3,8,16,768]{3,2,1,0:T(8,128)S(1)}, f32[3,8,16,768]{3,2,1,0:T(8,128)S(1)}, f32[16,768]{1,0:T(8,128)S(1)}) custom-call(f32[1,3,8,16,768]{4,3,2,1,0:T(8,128)} %ens.1, f32[2,8,16,768]{3,2,1,0:T(8,128)} %winds.1, f32[8]{0:T(128)} %diffusion_in.1, s32[16,768]{1,0:T(8,128)} %labels_in.1, f32[16]{0:T(128)} %amplitude_in.1), custom_call_target="tpu_custom_call" | custom-call | tf_op jit(solution)/shard_map/breed/pallas_call | solution.py:484
  49.2 1.2 %add_bitcast_fusion = f32[1,3,8,16,768]{4,3,2,1,0:T(8,128)} fusion(f32[3,8,16,768]{3,2,1,0:T(8,128)S(1)} %get-tuple-element.8, f32[3,8,16,768]{3,2,1,0:T(8,128)S(1)} %get-tuple-element.9, f32[16,768]{1,0:T(8,128)S(1)} %get-tuple-element.10), kind=kLoop, calls=%fused_computation | loop fusion | flops 589824 | bytes 3588096 | tf_op jit(solution)/shard_map/broadcast_in_dim | solution.py:514

commit v5 on v4

--- a/solution.py
+++ b/solution.py
@@ -339,9 +339,9 @@
         lax.fori_loop(0, levels - 1, one, 0)
 
     gather(1)
+    gather(2)
     other_levels(0)
     other_levels(1)
-    gather(2)
     other_levels(2)
 
     def blocks(v):

time: 50.6 us -> 50.4 us (level)
  Pallas kernels: 49.2 us -> 48.6 us
    pallas_call x1, Pallas kernels: 49.2 us -> 48.6 us  [on_device(): pl.pallas_call(kernel, name='breed', out_shape=(block, block, jax.ShapeDt...]
where the time goes in v5:
time: 50.4 us; the launch traced here: 49.8 us
  Pallas kernels  48.6 us (96%)
  other arithmetic  1.16 us (2%)
    pallas_call x1, Pallas kernels, on_device(): pl.pallas_call(kernel, name='breed', out_shape=(block, block, jax.ShapeDt...  48.6 us
    broadcast_in_dim x1, other arithmetic, on_device(): return (control + departure * scale)[None]  1.16 us

profile of v5, /device:TPU:56, one launch (start us, length us, event | category | flops | bytes accessed | tf_op | source)
XLA Modules:
  0.0 49.8 jit_solution(11112743302164202835)
XLA Ops:
  0.0 48.6 %breed.1 = (f32[3,8,16,768]{3,2,1,0:T(8,128)S(1)}, f32[3,8,16,768]{3,2,1,0:T(8,128)S(1)}, f32[16,768]{1,0:T(8,128)S(1)}) custom-call(f32[1,3,8,16,768]{4,3,2,1,0:T(8,128)} %ens.1, f32[2,8,16,768]{3,2,1,0:T(8,128)} %winds.1, f32[8]{0:T(128)} %diffusion_in.1, s32[16,768]{1,0:T(8,128)} %labels_in.1, f32[16]{0:T(128)} %amplitude_in.1), custom_call_target="tpu_custom_call" | custom-call | tf_op jit(solution)/shard_map/breed/pallas_call | solution.py:484
  48.6 1.2 %add_bitcast_fusion = f32[1,3,8,16,768]{4,3,2,1,0:T(8,128)} fusion(f32[3,8,16,768]{3,2,1,0:T(8,128)S(1)} %get-tuple-element.8, f32[3,8,16,768]{3,2,1,0:T(8,128)S(1)} %get-tuple-element.9, f32[16,768]{1,0:T(8,128)S(1)} %get-tuple-element.10), kind=kLoop, calls=%fused_computation | loop fusion | flops 589824 | bytes 3588096 | tf_op jit(solution)/shard_map/broadcast_in_dim | solution.py:514
